TPU v7x, 128 devices: a whole 4x4x4 slice. The times are simulated.
128 devices in a mesh: gx: 8 (over z, y_hi), bulk: 16 (over y_lo, x, core).
Axes of the slice: x: 4, y: 4 (y_hi: 2, y_lo: 2; y = y_hi * 2 + y_lo), z: 4, core: 2. Of those that a mesh axis runs over, the one named last changes fastest.
Arguments:
- saved_thermal_state: float32 [256, 512, 256], P('gx', 'bulk'), may hold values from -6 to 6
- thermal_diffusivity: float32 [256, 512, 256], P('gx', 'bulk'), may hold values from 0.25 to 1
- patch_power_density: float32 [1048576], P(('gx', 'bulk')), may hold values from -6 to 6
- entry_position: int32 [256, 512], P('gx', 'bulk'), may hold values from 0 to 1023
- incoming_patch_table: int32 [128, 128, 8], P(('gx', 'bulk')), may hold values from 0 to 8191
- terminal_sensitivity: float32 [256, 512, 256], P('gx', 'bulk'), may hold values from -6 to 6
Outputs:
- flux_grad: float32 [1048576], P(('gx', 'bulk'))
- start_adjoint: float32 [256, 512, 256], P('gx', 'bulk')
All inputs are finite; a program needn't handle non-finite values.
Results may differ from a plain program's by a relative error of at most 0.00002.
Values sent between devices are 32-bit elements; how exact they have to be, the bound alone decides.
A program may use at most 320 MiB of HBM per device.

v0:
```python
import jax
import jax.numpy as jnp
from jax import lax
from jax.experimental import pallas as pl
from jax.experimental.pallas import tpu as pltpu
from jax.sharding import PartitionSpec as P

MESH = pl.DeviceIdType.MESH
RATE = 0.08
DRIFT = 0.2
SOURCE = 0.5
HALF_RATE = 0.5 * RATE

NG, NB = 8, 16
CX, CY, CZ = 32, 32, 256

T0, DD, L3, T1, T2, L2, L1 = range(7)


def split3(x):
    hi = x.astype(jnp.bfloat16)
    rest = x - hi.astype(jnp.float32)
    mid = rest.astype(jnp.bfloat16)
    low = (rest - mid.astype(jnp.float32)).astype(jnp.bfloat16)
    return hi, mid, low


def iota(shape, axis):
    return lax.broadcasted_iota(jnp.int32, shape, axis)


def kernel(
    t0_hbm, d_hbm, l3_hbm, patch_ref, entry_ref, table_ref,
    flux_ref, adj_ref,
    fld, kay, slp, yrecv, ysend, kyh, rows, gath, hot_e, hot_p,
    load_sem, xs_sem, xr_sem, g_send, g_recv, b_send, b_recv,
):
    g = lax.axis_index("gx")
    b = lax.axis_index("bulk")

    loads = [
        pltpu.make_async_copy(src, fld.at[f, pl.ds(1, CX)], load_sem.at[f])
        for f, src in ((T0, t0_hbm), (DD, d_hbm), (L3, l3_hbm))
    ]
    for load in loads:
        load.start()
    barrier = pltpu.get_barrier_semaphore()
    for k in range(1, NG):
        pl.semaphore_signal(barrier, inc=1, device_id=(lax.rem(g + k, NG), b), device_id_type=MESH)
    for k in range(1, NB):
        pl.semaphore_signal(barrier, inc=1, device_id=(g, lax.rem(b + k, NB)), device_id_type=MESH)

    lane = iota((8, 128), 1)
    sub = iota((8, 128), 0)

    def stage_one(n, block):
        for o in range(NG):
            rows[n, 0, o] = block[o:o + 1, :]
        copies = []
        for k in range(1, NG):
            o = lax.rem(g + k, NG)
            c = pltpu.make_async_remote_copy(
                src_ref=rows.at[n, 0, o], dst_ref=rows.at[n, 1, g],
                send_sem=g_send.at[n, k], recv_sem=g_recv.at[n, k],
                device_id=(o, b), device_id_type=MESH)
            c.start()
            copies.append(c)
        rows[n, 1, g] = rows[n, 0, g]
        return copies

    def stage_two(n, first):
        for c in first:
            c.wait_recv()
        gath[n, b] = jnp.concatenate([rows[n, 1, o] for o in range(NG)], axis=0)
        copies = []
        for k in range(1, NB):
            c = pltpu.make_async_remote_copy(
                src_ref=gath.at[n, b], dst_ref=gath.at[n, b],
                send_sem=b_send.at[n, k], recv_sem=b_recv.at[n, k],
                device_id=(g, lax.rem(b + k, NB)), device_id_type=MESH)
            c.start()
            copies.append(c)
        return copies

    def finish(n, second):
        for c in second:
            c.wait_recv()
        out = jnp.zeros((8, 128), jnp.float32)
        for s in range(NB):
            turned = pltpu.roll(gath[n, s], lax.rem(s - b + 128, 128), axis=1)
            out = out + jnp.where((lane & 15) == s, turned, 0.0)
        return out

    def make_hot(hot, low):
        for q in range(8):
            hit = iota((128, 128), 0) == low[q:q + 1, :]
            hot[:, q * 128:(q + 1) * 128] = jnp.where(hit, 1.0, 0.0).astype(jnp.bfloat16)

    def lookup(parts, hot, high, count):
        stacked = jnp.concatenate(parts, axis=0)
        found = jnp.dot(stacked, hot[...], preferred_element_type=jnp.float32)
        total = found[:count] + found[count:2 * count] + found[2 * count:]
        out = []
        for q in range(8):
            piece = total[:, q * 128:(q + 1) * 128]
            hit = iota((count, 128), 0) == high[q:q + 1, :]
            out.append(jnp.sum(jnp.where(hit, piece, 0.0), axis=0, keepdims=True))
        return jnp.concatenate(out, axis=0)

    def scatter(values, hot, high, count):
        spread = jnp.concatenate(
            [jnp.where(iota((count, 128), 0) == high[q:q + 1, :], values[q:q + 1, :], 0.0)
             for q in range(8)], axis=1)
        total = jnp.zeros((count, 128), jnp.float32)
        for part in split3(spread):
            total = total + lax.dot_general(
                part, hot[...], (((1,), (1,)), ((), ())), preferred_element_type=jnp.float32)
        return total

    table = table_ref[...].astype(jnp.float32)
    listed = jnp.zeros((8, 128), jnp.float32)
    for k in range(8):
        turned = pltpu.roll(table, 16 * k, axis=1) if k else table
        kept = jnp.where((lane >> 4) == sub, turned, 0.0)
        listed = listed + (pltpu.roll(kept, 8 - k, axis=0) if k else kept)

    def zero_edges():
        for edge, plane, side in ((g == 0, 0, None), (g == NG - 1, CX + 1, None),
                                  (b == 0, None, 0), (b == NB - 1, None, 1)):
            @pl.when(edge)
            def _():
                for f in range(7):
                    if plane is not None:
                        fld[f, plane] = jnp.zeros((CY, CZ), jnp.float32)
                    else:
                        yrecv[f, side] = jnp.zeros((CX, CZ), jnp.float32)

    def faces(f):
        def remote(src, dst, way, target):
            return pltpu.make_async_remote_copy(
                src_ref=src, dst_ref=dst, send_sem=xs_sem.at[f, way], recv_sem=xr_sem.at[f, way],
                device_id=target, device_id_type=MESH)
        return (
            (g > 0, g < NG - 1, remote(fld.at[f, 1], fld.at[f, CX + 1], 0, (lax.max(g - 1, 0), b))),
            (g < NG - 1, g > 0, remote(fld.at[f, CX], fld.at[f, 0], 1, (lax.min(g + 1, NG - 1), b))),
            (b > 0, b < NB - 1, remote(ysend.at[f, 0], yrecv.at[f, 1], 2, (g, lax.max(b - 1, 0)))),
            (b < NB - 1, b > 0, remote(ysend.at[f, 1], yrecv.at[f, 0], 3, (g, lax.min(b + 1, NB - 1)))),
        )

    def pack(f):
        def body(x, _):
            ysend[f, 0, pl.ds(x, 1), :] = fld[f, x + 1, 0:1, :]
            ysend[f, 1, pl.ds(x, 1), :] = fld[f, x + 1, CY - 1:CY, :]
            return 0
        lax.fori_loop(0, CX, body, 0)

    def send(f):
        for sends, _, c in faces(f):
            @pl.when(sends)
            def _():
                c.start()

    def arrive(f):
        for _, receives, c in faces(f):
            @pl.when(receives)
            def _():
                c.wait_recv()

    def sent(f):
        for sends, _, c in faces(f):
            @pl.when(sends)
            def _():
                c.wait_send()

    row = iota((CY, CZ), 0)
    col = iota((CY, CZ), 1)

    def y_low(a, edge):
        return jnp.where(row == 0, edge, pltpu.roll(a, 1, axis=0))

    def y_high(a, edge):
        return jnp.where(row == CY - 1, edge, pltpu.roll(a, CY - 1, axis=0))

    def k_low(a):
        return jnp.where(col == 0, 0.0, pltpu.roll(a, 1, axis=1))

    def k_high(a, edge):
        return jnp.where(col == CZ - 1, edge, pltpu.roll(a, CZ - 1, axis=1))

    def conduct(n, f):
        def body(x, _):
            h = jnp.tanh(fld[f, x])
            d = fld[DD, x] * HALF_RATE
            kay[n, x] = d + (0.5 * d) * h
            slp[n, x] = (0.5 * d) * (1.0 - h * h)
            return 0
        lax.fori_loop(1, CX + 1, body, 0)

    def conduct_halo(n, f):
        for x in (0, CX + 1):
            kay[n, x] = HALF_RATE * fld[DD, x] * (1.0 + 0.5 * jnp.tanh(fld[f, x]))
        for side in range(2):
            kyh[n, side] = HALF_RATE * yrecv[DD, side] * (1.0 + 0.5 * jnp.tanh(yrecv[f, side]))

    def forward(n, f, out):
        def body(x, flow_low):
            t, k = fld[f, x], kay[n, x]
            one = pl.ds(x - 1, 1)
            flow_high = (k + kay[n, x + 1]) * (fld[f, x + 1] - t)
            acc = (1.0 - DRIFT) * t + DRIFT * fld[f, x - 1] + (flow_high - flow_low)
            y_l = (k + y_low(k, kyh[n, 0, one, :])) * (t - y_low(t, yrecv[f, 0, one, :]))
            y_top = (k[CY - 1:CY] + kyh[n, 1, one, :]) * (yrecv[f, 1, one, :] - t[CY - 1:CY])
            acc = acc + (y_high(y_l, y_top) - y_l)
            k_l = (k + k_low(k)) * (t - k_low(t))
            acc = acc + (k_high(k_l, -(k * t)) - k_l)
            fld[out, x] = acc
            return flow_high
        first = (kay[n, 0] + kay[n, 1]) * (fld[f, 1] - fld[f, 0])
        lax.fori_loop(1, CX + 1, body, first)

    def reverse(n, f, lam, store):
        def body(x, carry):
            g_x, m_x = carry
            t, k, l = fld[f, x], kay[n, x], fld[lam, x]
            one = pl.ds(x - 1, 1)
            l_up = fld[lam, x + 1]
            w = l - l_up
            g_u = w * (fld[f, x + 1] - t)
            m_u = w * (k + kay[n, x + 1])
            bend = g_x + g_u
            acc = (1.0 - DRIFT) * l + DRIFT * l_up + (m_x - m_u)
            w = y_low(l, yrecv[lam, 0, one, :]) - l
            g_l = w * (t - y_low(t, yrecv[f, 0, one, :]))
            m_l = w * (k + y_low(k, kyh[n, 0, one, :]))
            last = slice(CY - 1, CY)
            w = l[last] - yrecv[lam, 1, one, :]
            g_t = w * (yrecv[f, 1, one, :] - t[last])
            m_t = w * (k[last] + kyh[n, 1, one, :])
            bend = bend + (g_l + y_high(g_l, g_t))
            acc = acc + (m_l - y_high(m_l, m_t))
            w = k_low(l) - l
            g_l = w * (t - k_low(t))
            m_l = w * (k + k_low(k))
            bend = bend + (g_l + k_high(g_l, -(l * t)))
            acc = acc + (m_l - k_high(m_l, l * k))
            store(x, acc + slp[n, x] * bend)
            return g_u, m_u
        w = fld[lam, 0] - fld[lam, 1]
        first = (w * (fld[f, 1] - fld[f, 0]), w * (kay[n, 0] + kay[n, 1]))
        lax.fori_loop(1, CX + 1, body, first)

    def into(f):
        def store(x, value):
            fld[f, x] = value
        return store

    def into_out(x, value):
        adj_ref[x - 1] = value

    def add_heat(f, columns):
        top = iota((CY, 128), 1) == 0
        for x in range(CX):
            c = columns[(x % 4) * CY:(x % 4 + 1) * CY, x // 4:x // 4 + 1]
            fld[f, x + 1, :, 0:128] = fld[f, x + 1, :, 0:128] + jnp.where(top, SOURCE * c, 0.0)

    def surface(f):
        wide = iota((128, 128), 1)
        total = jnp.zeros((128, 128), jnp.float32)
        for q in range(8):
            block = jnp.concatenate([fld[f, 4 * q + j + 1, :, 0:128] for j in range(4)], axis=0)
            total = total + jnp.where(wide == q, pltpu.roll(block, q, axis=1) if q else block, 0.0)
        return total.T[0:8, :]

    zero_edges()
    pl.semaphore_wait(barrier, NG - 1 + NB - 1)
    a_first = stage_one(0, listed)
    loads[0].wait()
    pack(T0)
    send(T0)
    loads[1].wait()
    pack(DD)
    send(DD)
    conduct(0, T0)
    a_second = stage_two(0, a_first)
    loads[2].wait()
    pack(L3)
    send(L3)

    entry = entry_ref[...]
    e_high = entry >> 7
    make_hot(hot_e, ((entry & 7) << 4) + ((entry >> 3) & 15))
    patches = split3(patch_ref[...])

    spot = finish(0, a_second).astype(jnp.int32)
    p_high = spot >> 7
    make_hot(hot_p, spot & 127)
    v_first = stage_one(1, lookup(patches, hot_p, p_high, 64))

    arrive(T0)
    arrive(DD)
    conduct_halo(0, T0)
    v_second = stage_two(1, v_first)
    forward(0, T0, T1)
    heat = lookup(split3(finish(1, v_second)), hot_e, e_high, 8)
    columns = jnp.transpose(heat)
    add_heat(T1, columns)
    pack(T1)
    send(T1)
    conduct(1, T1)
    arrive(T1)
    conduct_halo(1, T1)
    forward(1, T1, T2)
    add_heat(T2, columns)
    pack(T2)
    send(T2)
    conduct(2, T2)
    arrive(T2)
    conduct_halo(2, T2)
    arrive(L3)
    reverse(2, T2, L3, into(L2))
    pack(L2)
    send(L2)
    arrive(L2)
    reverse(1, T1, L2, into(L1))
    pack(L1)
    send(L1)
    total = surface(L3) + surface(L2) + surface(L1)
    slots = scatter(SOURCE * total, hot_e, e_high, 8)
    c_first = stage_one(2, slots)
    arrive(L1)
    c_second = stage_two(2, c_first)
    reverse(0, T0, L1, into_out)
    flux_ref[...] = scatter(finish(2, c_second), hot_p, p_high, 64)

    for copies in (a_first, a_second, v_first, v_second, c_first, c_second):
        for c in copies:
            c.wait_send()
    for f in range(7):
        sent(f)


def shards(state, diffusivity, patches, entries, table, sensitivity):
    anywhere = pl.BlockSpec(memory_space=pl.ANY)
    vmem = pl.BlockSpec(memory_space=pltpu.VMEM)
    f32, bf16 = jnp.float32, jnp.bfloat16
    flux, adjoint = pl.pallas_call(
        kernel,
        out_shape=(
            jax.ShapeDtypeStruct((64, 128), f32),
            jax.ShapeDtypeStruct((CX, CY, CZ), f32),
        ),
        in_specs=[anywhere, anywhere, anywhere, vmem, vmem, vmem],
        out_specs=(vmem, vmem),
        scratch_shapes=[
            pltpu.VMEM((7, CX + 2, CY, CZ), f32),
            pltpu.VMEM((3, CX + 2, CY, CZ), f32),
            pltpu.VMEM((3, CX + 2, CY, CZ), f32),
            pltpu.VMEM((7, 2, CX, CZ), f32),
            pltpu.VMEM((7, 2, CX, CZ), f32),
            pltpu.VMEM((3, 2, CX, CZ), f32),
            pltpu.VMEM((3, 2, NG, 1, 128), f32),
            pltpu.VMEM((3, NB, 8, 128), f32),
            pltpu.VMEM((128, 1024), bf16),
            pltpu.VMEM((128, 1024), bf16),
            pltpu.SemaphoreType.DMA((3,)),
            pltpu.SemaphoreType.DMA((7, 4)),
            pltpu.SemaphoreType.DMA((7, 4)),
            pltpu.SemaphoreType.DMA((3, NG)),
            pltpu.SemaphoreType.DMA((3, NG)),
            pltpu.SemaphoreType.DMA((3, NB)),
            pltpu.SemaphoreType.DMA((3, NB)),
        ],
        compiler_params=pltpu.CompilerParams(
            collective_id=0, has_side_effects=True, vmem_limit_bytes=48 * 1024 * 1024),
    )(
        state, diffusivity, sensitivity, patches.reshape(64, 128),
        entries.reshape(8, 128), jnp.swapaxes(table[0], 0, 1),
    )
    return flux.reshape(-1), adjoint


def solution(mesh):
    return jax.shard_map(
        shards,
        mesh=mesh,
        in_specs=(
            P("gx", "bulk", None),
            P("gx", "bulk", None),
            P(("gx", "bulk")),
            P("gx", "bulk"),
            P(("gx", "bulk"), None, None),
            P("gx", "bulk", None),
        ),
        out_specs=(P(("gx", "bulk")), P("gx", "bulk", None)),
        check_vma=False,
    )
```

profile of v0, /device:TPU:0, one launch (start us, length us, event | category | flops | bytes accessed | tf_op | source)
XLA Modules:
  0.0 78.9 jit_solution(325254084085674749)
XLA Ops:
  0.6 0.0 copy-start.4
  0.6 0.8 %reshape.14.entry_ref = s32[8,128]{1,0:T(8,128)S(1)} reshape(s32[32,32]{1,0:T(8,128)} %param.9) | data formatting | bytes 8192 | tf_op jit(solution)/shard_map/reshape | solution.py:377
  1.4 0.0 copy-done.4
  1.4 0.0 copy-start
  1.4 1.2 %copy-done = f32[32,32,256]{2,1,0:T(8,128)S(1)} copy-done((f32[32,32,256]{2,1,0:T(8,128)S(1)}, f32[32,32,256]{2,1,0:T(8,128)}, u32[]{:S(2)}) %copy-start) | copy-done | bytes 1048600
  2.7 0.0 copy-start.1
  2.7 1.2 %copy-done.1 = f32[32,32,256]{2,1,0:T(8,128)S(1)} copy-done((f32[32,32,256]{2,1,0:T(8,128)S(1)}, f32[32,32,256]{2,1,0:T(8,128)}, u32[]{:S(2)}) %copy-start.1) | copy-done | bytes 1048600
  3.9 0.0 copy-start.2
  3.9 1.2 %copy-done.2 = f32[32,32,256]{2,1,0:T(8,128)S(1)} copy-done((f32[32,32,256]{2,1,0:T(8,128)S(1)}, f32[32,32,256]{2,1,0:T(8,128)}, u32[]{:S(2)}) %copy-start.2) | copy-done | bytes 1048600
  5.1 0.0 copy-start.3
  5.1 0.8 copy-done.3
  5.9 71.4 %shard_map.77 = (f32[64,128]{1,0:T(8,128)S(1)}, f32[32,32,256]{2,1,0:T(8,128)S(1)}) custom-call(f32[32,32,256]{2,1,0:T(8,128)S(1)} %copy-done, f32[32,32,256]{2,1,0:T(8,128)S(1)} %copy-done.1, f32[32,32,256]{2,1,0:T(8,128)S(1)} %copy-done.2, f32[64,128]{1,0:T(8,128)S(1)} %bitcast.5, s32[8,128]{1,0:T(8,128)S(1)} %reshape.14.entry_ref, s32[8,128]{1,0:T(8,128)S(1)} %bitcast.7), custom_call_target="tpu_custom_call" | custom-call | tf_op jit(solution)/shard_map/pallas_call | solution.py:346
  77.3 0.6 copy.10
  77.9 1.0 %copy.11 = f32[32,32,256]{2,1,0:T(8,128)} copy(f32[32,32,256]{2,1,0:T(8,128)S(1)} %get-tuple-element.9) | data formatting | bytes 2097152
Async XLA Ops:
  0.6 0.8 %copy-start.4 = (s32[1,128,8]{1,2,0:T(8,128)S(1)}, s32[1,128,8]{1,2,0:T(8,128)}, u32[]{:S(2)}) copy-start(s32[1,128,8]{1,2,0:T(8,128)} %param.10) | copy-start | bytes 12292
  1.4 1.2 %copy-start = (f32[32,32,256]{2,1,0:T(8,128)S(1)}, f32[32,32,256]{2,1,0:T(8,128)}, u32[]{:S(2)}) copy-start(f32[32,32,256]{2,1,0:T(8,128)} %t0_hbm.1) | copy-start | bytes 3145732
  2.7 1.2 %copy-start.1 = (f32[32,32,256]{2,1,0:T(8,128)S(1)}, f32[32,32,256]{2,1,0:T(8,128)}, u32[]{:S(2)}) copy-start(f32[32,32,256]{2,1,0:T(8,128)} %d_hbm.1) | copy-start | bytes 3145732
  3.9 1.2 %copy-start.2 = (f32[32,32,256]{2,1,0:T(8,128)S(1)}, f32[32,32,256]{2,1,0:T(8,128)}, u32[]{:S(2)}) copy-start(f32[32,32,256]{2,1,0:T(8,128)} %l3_hbm.1) | copy-start | bytes 3145732
  5.1 0.8 copy-start.3
where the time goes:
time: 79.2 us; the launch traced here: 78.9 us
  Pallas kernels  71.4 us (90%)
  local copies, waits for them, and re-layouts  6.82 us (9%)
    pallas_call x1, Pallas kernels, shards(): pl.pallas_call(kernel, out_shape=(jax.ShapeDtypeStruct((64, 128), f32), j...  71.4 us
    unnamed x12, local copies, waits for them, and re-layouts  6.02 us

commit v1 on v0

v1 whole, which is shorter than its diff:
```python
import jax
import jax.numpy as jnp
from jax import lax
from jax.experimental import pallas as pl
from jax.experimental.pallas import tpu as pltpu
from jax.sharding import PartitionSpec as P

MESH = pl.DeviceIdType.MESH
RATE = 0.08
DRIFT = 0.2
SOURCE = 0.5
HALF_RATE = 0.5 * RATE

NG, NB = 8, 16
CX, CY, CZ = 32, 32, 256

T0, DD, L3, T1, T2, L2, L1 = range(7)


def split3(x):
    hi = x.astype(jnp.bfloat16)
    rest = x - hi.astype(jnp.float32)
    mid = rest.astype(jnp.bfloat16)
    low = (rest - mid.astype(jnp.float32)).astype(jnp.bfloat16)
    return hi, mid, low


def iota(shape, axis):
    return lax.broadcasted_iota(jnp.int32, shape, axis)


def kernel(
    t0_hbm, d_hbm, l3_hbm, patch_ref, entry_ref, table_ref,
    flux_ref, adj_ref,
    fld, kay, slp, yrecv, ysend, kyh, kyf, syf, delta, outbox, inbox, hot_e, hot_p,
    load_sem, xs_sem, xr_sem, a_send, a_recv,
):
    g = lax.axis_index("gx")
    b = lax.axis_index("bulk")
    me = g * NB + b

    inputs = ((T0, t0_hbm), (DD, d_hbm), (L3, l3_hbm))
    edge_loads = [
        [pltpu.make_async_copy(src.at[:, y, :], ysend.at[f, side], load_sem.at[f, side])
         for side, y in ((0, 0), (1, CY - 1))]
        for f, src in inputs
    ]
    loads = [
        pltpu.make_async_copy(src, fld.at[f, pl.ds(1, CX)], load_sem.at[f, 2])
        for f, src in inputs
    ]
    for pair in edge_loads:
        for load in pair:
            load.start()
    for load in loads:
        load.start()
    barrier = pltpu.get_barrier_semaphore()

    def each_other(act):
        for j in range(1, NB):
            act(g, lax.rem(b + j, NB))

        def body(i, _):
            for j in range(NB):
                act(lax.rem(g + i, NG), lax.rem(b + j, NB))
            return 0
        lax.fori_loop(1, NG, body, 0)

    each_other(lambda tg, tb: pl.semaphore_signal(
        barrier, inc=1, device_id=(tg, tb), device_id_type=MESH))

    def post(n, block):
        outbox[n] = jnp.concatenate([block, jnp.zeros((120, 128), jnp.float32)], axis=0).T

        def act(tg, tb):
            pltpu.make_async_remote_copy(
                src_ref=outbox.at[n, pl.ds(tg * NB + tb, 1)], dst_ref=inbox.at[n, pl.ds(me, 1)],
                send_sem=a_send.at[n], recv_sem=a_recv.at[n],
                device_id=(tg, tb), device_id_type=MESH).start()
        each_other(act)
        inbox[n, pl.ds(me, 1)] = outbox[n, pl.ds(me, 1)]

    def everything(n):
        return pltpu.make_async_remote_copy(
            src_ref=outbox.at[n, pl.ds(0, NG * NB - 1)], dst_ref=inbox.at[n, pl.ds(0, NG * NB - 1)],
            send_sem=a_send.at[n], recv_sem=a_recv.at[n],
            device_id=(g, b), device_id_type=MESH)

    def collect(n):
        everything(n).wait_recv()
        return inbox[n].T[0:8]

    def make_hot(hot, low):
        for q in range(8):
            hit = iota((128, 128), 0) == low[q:q + 1, :]
            hot[:, q * 128:(q + 1) * 128] = jnp.where(hit, 1.0, 0.0).astype(jnp.bfloat16)

    def lookup(parts, hot, high, count):
        stacked = jnp.concatenate(parts, axis=0)
        found = jnp.dot(stacked, hot[...], preferred_element_type=jnp.float32)
        total = found[:count] + found[count:2 * count] + found[2 * count:]
        out = []
        for q in range(8):
            piece = total[:, q * 128:(q + 1) * 128]
            hit = iota((count, 128), 0) == high[q:q + 1, :]
            out.append(jnp.sum(jnp.where(hit, piece, 0.0), axis=0, keepdims=True))
        return jnp.concatenate(out, axis=0)

    def scatter(values, hot, high, count):
        spread = jnp.concatenate(
            [jnp.where(iota((count, 128), 0) == high[q:q + 1, :], values[q:q + 1, :], 0.0)
             for q in range(8)], axis=1)
        total = jnp.zeros((count, 128), jnp.float32)
        for part in split3(spread):
            total = total + lax.dot_general(
                part, hot[...], (((1,), (1,)), ((), ())), preferred_element_type=jnp.float32)
        return total

    def zero_edges():
        for edge, plane, side in ((g == 0, 0, None), (g == NG - 1, CX + 1, None),
                                  (b == 0, None, 0), (b == NB - 1, None, 1)):
            @pl.when(edge)
            def _():
                for f in range(7):
                    if plane is not None:
                        fld[f, plane] = jnp.zeros((CY, CZ), jnp.float32)
                    else:
                        yrecv[f, side] = jnp.zeros((CX, CZ), jnp.float32)

    def faces(f):
        def remote(src, dst, way, target):
            return pltpu.make_async_remote_copy(
                src_ref=src, dst_ref=dst, send_sem=xs_sem.at[f, way], recv_sem=xr_sem.at[f, way],
                device_id=target, device_id_type=MESH)
        return (
            (g > 0, g < NG - 1, remote(fld.at[f, 1], fld.at[f, CX + 1], 0, (lax.max(g - 1, 0), b))),
            (g < NG - 1, g > 0, remote(fld.at[f, CX], fld.at[f, 0], 1, (lax.min(g + 1, NG - 1), b))),
            (b > 0, b < NB - 1, remote(ysend.at[f, 0], yrecv.at[f, 1], 2, (g, lax.max(b - 1, 0)))),
            (b < NB - 1, b > 0, remote(ysend.at[f, 1], yrecv.at[f, 0], 3, (g, lax.min(b + 1, NB - 1)))),
        )

    def send(f):
        for sends, _, c in faces(f):
            @pl.when(sends)
            def _():
                c.start()

    def arrive(f):
        for _, receives, c in faces(f):
            @pl.when(receives)
            def _():
                c.wait_recv()

    def sent(f):
        for sends, _, c in faces(f):
            @pl.when(sends)
            def _():
                c.wait_send()

    row = iota((CY, CZ), 0)
    col = iota((CY, CZ), 1)

    def y_down(a):
        return pltpu.roll(a, 1, axis=0)

    def y_up(a):
        return pltpu.roll(a, CY - 1, axis=0)

    def k_down(a):
        return pltpu.roll(a, 1, axis=1)

    def k_up(a):
        return pltpu.roll(a, CZ - 1, axis=1)

    def planes(step, carry):
        carry = lax.fori_loop(1, CX - 3, lambda x, c: step(x, c, False), carry, unroll=4)
        for x in range(CX - 3, CX + 1):
            carry = step(x, carry, x == CX)

    def conduct(n, f):
        def body(x, _):
            h = jnp.tanh(fld[f, x])
            d = fld[DD, x] * HALF_RATE
            kay[n, x] = d + (0.5 * d) * h
            slp[n, x] = (0.5 * d) * (1.0 - h * h)
            return 0
        lax.fori_loop(1, CX + 1, body, 0, unroll=4)

    def conduct_own(n, f):
        for side in range(2):
            h = jnp.tanh(ysend[f, side])
            d = ysend[DD, side] * HALF_RATE
            kyf[n, side] = d + (0.5 * d) * h
            syf[n, side] = (0.5 * d) * (1.0 - h * h)

    def conduct_halo(n, f):
        for x in (0, CX + 1):
            kay[n, x] = HALF_RATE * fld[DD, x] * (1.0 + 0.5 * jnp.tanh(fld[f, x]))
        for side in range(2):
            kyh[n, side] = HALF_RATE * yrecv[DD, side] * (1.0 + 0.5 * jnp.tanh(yrecv[f, side]))

    def forward(n, f, out):
        def step(x, flow_low, last):
            t, k = fld[f, x], kay[n, x]
            acc = (1.0 - DRIFT) * t - flow_low[0] + flow_low[1]
            flow = None
            if not last:
                flow = (k + kay[n, x + 1]) * (fld[f, x + 1] - t)
                acc = acc + flow
            y_l = jnp.where(row == 0, 0.0, (k + y_down(k)) * (t - y_down(t)))
            acc = acc + (y_up(y_l) - y_l)
            kt = k * t
            k_l = jnp.where(col == 0, kt, (k + k_down(k)) * (t - k_down(t)))
            acc = acc + (jnp.where(col == CZ - 1, -kt, k_up(k_l)) - k_l)
            fld[out, x] = acc
            return flow, DRIFT * t
        zero = jnp.zeros((CY, CZ), jnp.float32)
        planes(step, (zero, zero))

    def forward_faces(n, f, out):
        low, high = fld[f, 0], fld[f, CX + 1]
        fld[out, 1] = fld[out, 1] + DRIFT * low - (kay[n, 0] + kay[n, 1]) * (fld[f, 1] - low)
        fld[out, CX] = fld[out, CX] + (kay[n, CX] + kay[n, CX + 1]) * (high - fld[f, CX])
        for side in range(2):
            delta[side] = (kyf[n, side] + kyh[n, side]) * (yrecv[f, side] - ysend[f, side])

    def reverse(n, f, lam, out):
        def step(x, carry, last):
            g_x, m_x = carry
            t, k, l = fld[f, x], kay[n, x], fld[lam, x]
            bend = g_x
            acc = (1.0 - DRIFT) * l + m_x
            g_u = m_u = None
            if not last:
                l_up = fld[lam, x + 1]
                w = l - l_up
                g_u = w * (fld[f, x + 1] - t)
                m_u = w * (k + kay[n, x + 1])
                bend = bend + g_u
                acc = acc + (DRIFT * l_up - m_u)
            w = jnp.where(row == 0, 0.0, y_down(l) - l)
            g_l = w * (t - y_down(t))
            m_l = w * (k + y_down(k))
            bend = bend + (g_l + y_up(g_l))
            acc = acc + (m_l - y_up(m_l))
            lt, lk = l * t, l * k
            w = k_down(l) - l
            g_l = jnp.where(col == 0, -lt, w * (t - k_down(t)))
            m_l = jnp.where(col == 0, -lk, w * (k + k_down(k)))
            bend = bend + (g_l + jnp.where(col == CZ - 1, -lt, k_up(g_l)))
            acc = acc + (m_l - jnp.where(col == CZ - 1, lk, k_up(m_l)))
            value = acc + slp[n, x] * bend
            if out is None:
                adj_ref[x - 1] = value
            else:
                fld[out, x] = value
            return g_u, m_u
        zero = jnp.zeros((CY, CZ), jnp.float32)
        planes(step, (zero, zero))

    def reverse_faces(n, f, lam, out):
        w = fld[lam, 0] - fld[lam, 1]
        low = (slp[n, 1] * (w * (fld[f, 1] - fld[f, 0])) + w * (kay[n, 0] + kay[n, 1]))
        w = fld[lam, CX] - fld[lam, CX + 1]
        high = (slp[n, CX] * (w * (fld[f, CX + 1] - fld[f, CX])) - w * (kay[n, CX] + kay[n, CX + 1])
                + DRIFT * fld[lam, CX + 1])
        if out is None:
            adj_ref[0] = adj_ref[0] + low
            adj_ref[CX - 1] = adj_ref[CX - 1] + high
        else:
            fld[out, 1] = fld[out, 1] + low
            fld[out, CX] = fld[out, CX] + high
        for side in range(2):
            w = yrecv[lam, side] - ysend[lam, side]
            bend = w * (ysend[f, side] - yrecv[f, side])
            delta[side] = syf[n, side] * bend + w * (kyf[n, side] + kyh[n, side])

    def add_delta(f):
        def body(x, _):
            for side, y in ((0, slice(0, 1)), (1, slice(CY - 1, CY))):
                if f is None:
                    adj_ref[x, y] = adj_ref[x, y] + delta[side, pl.ds(x, 1), :]
                else:
                    new = fld[f, x + 1, y] + delta[side, pl.ds(x, 1), :]
                    fld[f, x + 1, y] = new
                    ysend[f, side, pl.ds(x, 1), :] = new
            return 0
        lax.fori_loop(0, CX, body, 0, unroll=4)

    def add_heat(f, columns):
        top = iota((CY, 128), 1) == 0
        for x in range(CX):
            c = columns[(x % 4) * CY:(x % 4 + 1) * CY, x // 4:x // 4 + 1]
            fld[f, x + 1, :, 0:128] = fld[f, x + 1, :, 0:128] + jnp.where(top, SOURCE * c, 0.0)

    def surface(f):
        wide = iota((128, 128), 1)
        total = jnp.zeros((128, 128), jnp.float32)
        for q in range(8):
            block = jnp.concatenate([fld[f, 4 * q + j + 1, :, 0:128] for j in range(4)], axis=0)
            total = total + jnp.where(wide == q, pltpu.roll(block, q, axis=1) if q else block, 0.0)
        return total.T[0:8, :]

    zero_edges()
    table = table_ref[...].astype(jnp.float32)
    pl.semaphore_wait(barrier, NG * NB - 1)
    post(0, table)
    for i, f in ((0, T0), (1, DD), (2, L3)):
        for load in edge_loads[i]:
            load.wait()
        loads[i].wait()
        send(f)
    conduct(0, T0)
    conduct_own(0, T0)
    patches = split3(patch_ref[...])

    spot = collect(0).astype(jnp.int32)
    p_high = spot >> 7
    make_hot(hot_p, spot & 127)
    post(1, lookup(patches, hot_p, p_high, 64))

    forward(0, T0, T1)
    arrive(T0)
    arrive(DD)
    conduct_halo(0, T0)
    forward_faces(0, T0, T1)
    entry = jnp.concatenate([entry_ref[pl.ds(j, 8, stride=4), :] for j in range(4)], axis=1)
    e_high = entry & 7
    make_hot(hot_e, entry >> 3)
    heat = lookup(split3(collect(1)), hot_e, e_high, 8)
    columns = jnp.transpose(heat)
    add_heat(T1, columns)
    add_delta(T1)
    send(T1)
    conduct(1, T1)
    conduct_own(1, T1)
    forward(1, T1, T2)
    add_heat(T2, columns)
    arrive(T1)
    conduct_halo(1, T1)
    forward_faces(1, T1, T2)
    add_delta(T2)
    send(T2)
    conduct(2, T2)
    conduct_own(2, T2)
    reverse(2, T2, L3, L2)
    arrive(L3)
    arrive(T2)
    conduct_halo(2, T2)
    reverse_faces(2, T2, L3, L2)
    add_delta(L2)
    send(L2)
    reverse(1, T1, L2, L1)
    total = surface(L3) + surface(L2)
    arrive(L2)
    reverse_faces(1, T1, L2, L1)
    add_delta(L1)
    send(L1)
    total = total + surface(L1)
    post(2, scatter(SOURCE * total, hot_e, e_high, 8))
    reverse(0, T0, L1, None)
    arrive(L1)
    reverse_faces(0, T0, L1, None)
    add_delta(None)
    flux_ref[...] = scatter(collect(2), hot_p, p_high, 64)

    for n in range(3):
        everything(n).wait_send()
    for f in range(7):
        sent(f)


def shards(state, diffusivity, patches, entries, table, sensitivity):
    anywhere = pl.BlockSpec(memory_space=pl.ANY)
    vmem = pl.BlockSpec(memory_space=pltpu.VMEM)
    f32, bf16 = jnp.float32, jnp.bfloat16
    flux, adjoint = pl.pallas_call(
        kernel,
        out_shape=(
            jax.ShapeDtypeStruct((64, 128), f32),
            jax.ShapeDtypeStruct((CX, CY, CZ), f32),
        ),
        in_specs=[anywhere, anywhere, anywhere, vmem, vmem, vmem],
        out_specs=(vmem, vmem),
        scratch_shapes=[
            pltpu.VMEM((7, CX + 2, CY, CZ), f32),
            pltpu.VMEM((3, CX + 2, CY, CZ), f32),
            pltpu.VMEM((3, CX + 2, CY, CZ), f32),
            pltpu.VMEM((7, 2, CX, CZ), f32),
            pltpu.VMEM((7, 2, CX, CZ), f32),
            pltpu.VMEM((3, 2, CX, CZ), f32),
            pltpu.VMEM((3, 2, CX, CZ), f32),
            pltpu.VMEM((3, 2, CX, CZ), f32),
            pltpu.VMEM((2, CX, CZ), f32),
            pltpu.VMEM((3, NG * NB, 128), f32),
            pltpu.VMEM((3, NG * NB, 128), f32),
            pltpu.VMEM((128, 1024), bf16),
            pltpu.VMEM((128, 1024), bf16),
            pltpu.SemaphoreType.DMA((3, 3)),
            pltpu.SemaphoreType.DMA((7, 4)),
            pltpu.SemaphoreType.DMA((7, 4)),
            pltpu.SemaphoreType.DMA((3,)),
            pltpu.SemaphoreType.DMA((3,)),
        ],
        compiler_params=pltpu.CompilerParams(
            collective_id=0, has_side_effects=True, vmem_limit_bytes=63 * 1024 * 1024),
    )(
        state, diffusivity, sensitivity, patches.reshape(64, 128),
        entries, jnp.swapaxes(table[0], 0, 1),
    )
    return flux.reshape(-1), adjoint


def solution(mesh):
    return jax.shard_map(
        shards,
        mesh=mesh,
        in_specs=(
            P("gx", "bulk", None),
            P("gx", "bulk", None),
            P(("gx", "bulk")),
            P("gx", "bulk"),
            P(("gx", "bulk"), None, None),
            P("gx", "bulk", None),
        ),
        out_specs=(P(("gx", "bulk")), P("gx", "bulk", None)),
        check_vma=False,
    )
```

time: 79.2 us -> 50.8 us (0.64)
  the two profiles are of different devices: /device:TPU:0 before, /device:TPU:1 now
where the time goes in v1:
time: 50.8 us; the launch traced here: 50.5 us
  Pallas kernels  46.2 us (91%)
  local copies, waits for them, and re-layouts  3.68 us (7%)
  between operations  0.64 us (1%)
    pallas_call x1, Pallas kernels, shards(): pl.pallas_call(kernel, out_shape=(jax.ShapeDtypeStruct((64, 128), f32), j...  46.2 us
    unnamed x2, local copies, waits for them, and re-layouts  3.68 us

profile of v1, /device:TPU:1, one launch (start us, length us, event | category | flops | bytes accessed | tf_op | source)
XLA Modules:
  0.0 50.5 jit_solution(11404109337321635194)
XLA Ops:
  0.6 46.2 %shard_map.77 = (f32[64,128]{1,0:T(8,128)}, f32[32,32,256]{2,1,0:T(8,128)}) custom-call(f32[32,32,256]{2,1,0:T(8,128)} %t0_hbm.1, f32[32,32,256]{2,1,0:T(8,128)} %d_hbm.1, f32[32,32,256]{2,1,0:T(8,128)} %l3_hbm.1, f32[64,128]{1,0:T(8,128)} %bitcast.5, s32[32,32]{1,0:T(8,128)} %entry_ref.1, s32[8,128]{1,0:T(8,128)} %bitcast.7), custom_call_target="tpu_custom_call" | custom-call | tf_op jit(solution)/shard_map/pallas_call | solution.py:377
  46.8 1.4 %copy.10 = f32[8192]{0:T(1024)} copy(f32[8192]{0:T(1024)} %bitcast.6) | data formatting | bytes 65536
  48.2 2.3 %copy.11 = f32[32,32,256]{2,1,0:T(8,128)} copy(f32[32,32,256]{2,1,0:T(8,128)} %get-tuple-element.9) | data formatting | bytes 2097152

commit v2 on v1

--- a/solution.py
+++ b/solution.py
@@ -16,6 +16,11 @@
 
 T0, DD, L3, T1, T2, L2, L1 = range(7)
 
+WY = CY + 16
+TR = 6 * WY
+TL = 384
+KAY0, SLP0, TEM1, LAM1, LAM0 = range(5)
+
 
 def split3(x):
     hi = x.astype(jnp.bfloat16)
@@ -32,8 +37,8 @@
 def kernel(
     t0_hbm, d_hbm, l3_hbm, patch_ref, entry_ref, table_ref,
     flux_ref, adj_ref,
-    fld, kay, slp, yrecv, ysend, kyh, kyf, syf, delta, outbox, inbox, hot_e, hot_p,
-    load_sem, xs_sem, xr_sem, a_send, a_recv,
+    fld, kay, slp, yrecv, ysend, kyh, kyf, syf, delta, outbox, inbox, hot_n, hot_p, top, nst, turn,
+    load_sem, xs_sem, xr_sem, a_send, a_recv, t_send, t_recv,
 ):
     g = lax.axis_index("gx")
     b = lax.axis_index("bulk")
@@ -70,7 +75,8 @@
         barrier, inc=1, device_id=(tg, tb), device_id_type=MESH))
 
     def post(n, block):
-        outbox[n] = jnp.concatenate([block, jnp.zeros((120, 128), jnp.float32)], axis=0).T
+        pad = jnp.zeros((128 - block.shape[0], 128), jnp.float32)
+        outbox[n] = jnp.concatenate([block, pad], axis=0).T
 
         def act(tg, tb):
             pltpu.make_async_remote_copy(
@@ -86,9 +92,9 @@
             send_sem=a_send.at[n], recv_sem=a_recv.at[n],
             device_id=(g, b), device_id_type=MESH)
 
-    def collect(n):
+    def collect(n, count):
         everything(n).wait_recv()
-        return inbox[n].T[0:8]
+        return inbox[n].T[0:count]
 
     def make_hot(hot, low):
         for q in range(8):
@@ -287,19 +293,178 @@
             return 0
         lax.fori_loop(0, CX, body, 0, unroll=4)
 
-    def add_heat(f, columns):
-        top = iota((CY, 128), 1) == 0
+    wide = iota((TR, 128), 1)
+    tall = iota((TR, 128), 0)
+    strip = (tall * 1366) >> 16
+    inside = tall - WY * strip
+    outside = (
+        ((strip == 0) & (g == 0)) | ((strip == 5) & (g == NG - 1))
+        | ((inside < 8) & (b == 0)) | ((inside >= 8 + CY) & (b == NB - 1))
+    )
+    surface = (wide & 15) == 0
+
+    def in_grid(a):
+        return jnp.where(outside, 0.0, a)
+
+    def next_x(a):
+        r = pltpu.roll(a, 112, axis=1)
+        return jnp.where(wide < 112, r, jnp.concatenate([r[WY:], r[:WY]], axis=0))
+
+    def last_x(a):
+        r = pltpu.roll(a, 16, axis=1)
+        return jnp.where(wide >= 16, r, jnp.concatenate([r[TR - WY:], r[:TR - WY]], axis=0))
+
+    def next_y(a):
+        return pltpu.roll(a, TR - 1, axis=0)
+
+    def last_y(a):
+        return pltpu.roll(a, 1, axis=0)
+
+    def next_k(a):
+        return pltpu.roll(a, 127, axis=1)
+
+    def last_k(a):
+        return pltpu.roll(a, 1, axis=1)
+
+    def top_conduct(t, d):
+        h = jnp.tanh(t)
+        d = d * HALF_RATE
+        return d + (0.5 * d) * h, (0.5 * d) * (1.0 - h * h)
+
+    def top_forward(t, k):
+        flow = (k + next_x(k)) * (next_x(t) - t)
+        acc = (1.0 - DRIFT) * t + DRIFT * last_x(t) + (flow - last_x(flow))
+        flow = (k + next_y(k)) * (next_y(t) - t)
+        acc = acc + (flow - last_y(flow))
+        flow = jnp.where(surface, k * t, (k + last_k(k)) * (t - last_k(t)))
+        return acc + (next_k(flow) - flow)
+
+    def top_reverse(t, k, s, l):
+        l_up = next_x(l)
+        w = l - l_up
+        bent = w * (next_x(t) - t)
+        moved = w * (k + next_x(k))
+        bend = bent + last_x(bent)
+        acc = (1.0 - DRIFT) * l + DRIFT * l_up + (last_x(moved) - moved)
+        w = l - next_y(l)
+        bent = w * (next_y(t) - t)
+        moved = w * (k + next_y(k))
+        bend = bend + (bent + last_y(bent))
+        acc = acc + (last_y(moved) - moved)
+        w = last_k(l) - l
+        bent = jnp.where(surface, -(l * t), w * (t - last_k(t)))
+        moved = jnp.where(surface, -(l * k), w * (k + last_k(k)))
+        bend = bend + (bent + next_k(bent))
+        acc = acc + (moved - next_k(moved))
+        return in_grid(acc + s * bend)
+
+    def top_pack():
+        lane = iota((CY, 128), 1) >> 4
+        for i, f in enumerate((T0, DD, L3)):
+            for strip_x in range(4):
+                x = 1 + 8 * strip_x
+                tile = fld[f, x, :, 0:128]
+                for j in range(1, 8):
+                    tile = jnp.where(lane == j, pltpu.roll(fld[f, x + j, :, 0:128], 16 * j, axis=1), tile)
+                top[i, 1 + strip_x, 8:8 + CY] = tile
+        entry = jnp.concatenate([entry_ref[...], jnp.zeros((CX, 128 - CY), jnp.int32)], axis=1)
+        entry = jnp.concatenate([entry.astype(jnp.float32), jnp.zeros((128 - CX, 128), jnp.float32)], axis=0)
+        entry = entry.T[0:CY].astype(jnp.int32)
+        spread = jnp.where(iota((128, 512), 0) == (iota((128, 512), 1) >> 4), 1.0, 0.0).astype(jnp.bfloat16)
+        high = jnp.dot((entry >> 3).astype(jnp.float32).astype(jnp.bfloat16), spread,
+                       preferred_element_type=jnp.float32)
+        low = jnp.dot((entry & 7).astype(jnp.float32).astype(jnp.bfloat16), spread,
+                      preferred_element_type=jnp.float32)
+        entry = 8.0 * high + low
+        for strip_x in range(4):
+            top[3, 1 + strip_x, 8:8 + CY] = entry[:, 128 * strip_x:128 * (strip_x + 1)]
+
+    def top_copies():
+        out = []
+        along_x = {-1: (1, 1, 5), 0: (1, 4, 1), 1: (4, 1, 0)}
+        along_y = {-1: (8, 8, 8 + CY), 0: (8, CY, 8), 1: (CY, 8, 0)}
+        for dx in (-1, 0, 1):
+            for dy in (-1, 0, 1):
+                if dx == 0 and dy == 0:
+                    continue
+                way = (dx + 1) * 3 + dy + 1
+                x, wide_x, to_x = along_x[dx]
+                y, wide_y, to_y = along_y[dy]
+                sends, receives = None, None
+                for d, at, size in ((dx, g, NG), (dy, b, NB)):
+                    if d:
+                        one = (at > 0, at < size - 1)
+                        one = one if d < 0 else one[::-1]
+                        sends = one[0] if sends is None else sends & one[0]
+                        receives = one[1] if receives is None else receives & one[1]
+                target = (lax.clamp(0, g + dx, NG - 1), lax.clamp(0, b + dy, NB - 1))
+                out.append((sends, receives, pltpu.make_async_remote_copy(
+                    src_ref=top.at[:, pl.ds(x, wide_x), pl.ds(y, wide_y)],
+                    dst_ref=top.at[:, pl.ds(to_x, wide_x), pl.ds(to_y, wide_y)],
+                    send_sem=t_send.at[way], recv_sem=t_recv.at[way],
+                    device_id=target, device_id_type=MESH)))
+        return out
+
+    def when(condition, action):
+        @pl.when(condition)
+        def _():
+            action()
+
+    line = iota((1, TL), 1)
+    line_strip = (line * 1366) >> 16
+    line_y = line - WY * line_strip
+    side_x = jnp.where(line_strip == 0, 0, jnp.where(line_strip >= 5, 2, 1))
+    side_y = jnp.where(line_y < 8, 0, jnp.where(line_y >= 8 + CY, 2, 1))
+    whose = 3 * side_x + side_y
+    ours = whose == 4
+
+    def to_lines(a):
+        turned = jnp.concatenate([a, jnp.zeros((TL - TR, 128), jnp.float32)], axis=0).T
+        return jnp.concatenate([turned[16 * j:16 * j + 1] for j in range(8)], axis=0)
+
+    def from_lines(lines):
+        turn[...] = jnp.zeros((128, TL), jnp.float32)
+        for j in range(8):
+            turn[16 * j:16 * j + 1, :] = lines[j]
+        return turn[...].T[0:TR]
+
+    def neighbours(v):
+        return jnp.concatenate(
+            [pltpu.roll(v, (-(NB * dx + dy)) % 128, axis=1) if dx or dy else v
+             for dx in (-1, 0, 1) for dy in (-1, 0, 1)], axis=0)
+
+    def top_hot(entry):
+        for j in range(8):
+            hit = iota((128, TL), 0) == (entry[j:j + 1] >> 3)
+            hot_n[:, j * TL:(j + 1) * TL] = jnp.where(hit, 1.0, 0.0).astype(jnp.bfloat16)
+
+    def top_heat(slots, entry):
+        stacked = jnp.concatenate(split3(slots), axis=0)
+        lines = []
+        for j in range(8):
+            found = jnp.dot(stacked, hot_n[:, j * TL:(j + 1) * TL], preferred_element_type=jnp.float32)
+            found = found[:72] + found[72:144] + found[144:]
+            hit = iota((72, TL), 0) == 8 * whose + (entry[j:j + 1] & 7)
+            lines.append(jnp.sum(jnp.where(hit, found, 0.0), axis=0, keepdims=True))
+        return from_lines(lines)
+
+    def top_slots(a, entry):
+        lines = to_lines(a)
+        spread = jnp.concatenate(
+            [jnp.where((iota((8, TL), 0) == (entry[j:j + 1] & 7)) & ours, lines[j:j + 1], 0.0)
+             for j in range(8)], axis=1)
+        stacked = jnp.concatenate(split3(spread), axis=0)
+        total = lax.dot_general(
+            stacked, hot_n[...], (((1,), (1,)), ((), ())), preferred_element_type=jnp.float32)
+        return total[0:8] + total[8:16] + total[16:24]
+
+    def overlay():
+        lane = iota((CY, 128), 1)
         for x in range(CX):
-            c = columns[(x % 4) * CY:(x % 4 + 1) * CY, x // 4:x // 4 + 1]
-            fld[f, x + 1, :, 0:128] = fld[f, x + 1, :, 0:128] + jnp.where(top, SOURCE * c, 0.0)
-
-    def surface(f):
-        wide = iota((128, 128), 1)
-        total = jnp.zeros((128, 128), jnp.float32)
-        for q in range(8):
-            block = jnp.concatenate([fld[f, 4 * q + j + 1, :, 0:128] for j in range(4)], axis=0)
-            total = total + jnp.where(wide == q, pltpu.roll(block, q, axis=1) if q else block, 0.0)
-        return total.T[0:8, :]
+            rows = nst[LAM0, (1 + x // 8) * WY + 8:(1 + x // 8) * WY + 8 + CY]
+            j = x % 8
+            rows = pltpu.roll(rows, 128 - 16 * j, axis=1) if j else rows
+            adj_ref[x, :, 0:128] = jnp.where(lane < 5, rows, adj_ref[x, :, 0:128])
 
     zero_edges()
     table = table_ref[...].astype(jnp.float32)
@@ -310,37 +475,57 @@
             load.wait()
         loads[i].wait()
         send(f)
+    top_pack()
+    tops = top_copies()
+    for sends, _, c in tops:
+        when(sends, c.start)
     conduct(0, T0)
     conduct_own(0, T0)
     patches = split3(patch_ref[...])
 
-    spot = collect(0).astype(jnp.int32)
+    spot = collect(0, 8).astype(jnp.int32)
     p_high = spot >> 7
     make_hot(hot_p, spot & 127)
-    post(1, lookup(patches, hot_p, p_high, 64))
+    post(1, neighbours(lookup(patches, hot_p, p_high, 64)))
 
     forward(0, T0, T1)
     arrive(T0)
     arrive(DD)
     conduct_halo(0, T0)
     forward_faces(0, T0, T1)
-    entry = jnp.concatenate([entry_ref[pl.ds(j, 8, stride=4), :] for j in range(4)], axis=1)
-    e_high = entry & 7
-    make_hot(hot_e, entry >> 3)
-    heat = lookup(split3(collect(1)), hot_e, e_high, 8)
-    columns = jnp.transpose(heat)
-    add_heat(T1, columns)
     add_delta(T1)
     send(T1)
     conduct(1, T1)
     conduct_own(1, T1)
     forward(1, T1, T2)
-    add_heat(T2, columns)
+
+    for _, receives, c in tops:
+        when(receives, c.wait_recv)
+    def whole(i):
+        return top[i].reshape(TR, 128)
+    t0, d, l3 = in_grid(whole(0)), in_grid(whole(1)), in_grid(whole(2))
+    entry = to_lines(whole(3)).astype(jnp.int32)
+    top_hot(entry)
+    k0, s0 = top_conduct(t0, d)
+    nst[KAY0], nst[SLP0] = k0, s0
+    nst[TEM1] = top_forward(t0, k0)
+
     arrive(T1)
     conduct_halo(1, T1)
     forward_faces(1, T1, T2)
     add_delta(T2)
     send(T2)
+
+    heat = SOURCE * top_heat(collect(1, 72), entry)
+    t1 = in_grid(nst[TEM1] + heat)
+    k1, s1 = top_conduct(t1, d)
+    t2 = in_grid(top_forward(t1, k1) + heat)
+    k2, s2 = top_conduct(t2, d)
+    l2 = top_reverse(t2, k2, s2, l3)
+    l1 = top_reverse(t1, k1, s1, l2)
+    post(2, top_slots(SOURCE * (l3 + l2 + l1), entry))
+    nst[LAM1] = l1
+
     conduct(2, T2)
     conduct_own(2, T2)
     reverse(2, T2, L3, L2)
@@ -350,24 +535,25 @@
     reverse_faces(2, T2, L3, L2)
     add_delta(L2)
     send(L2)
+    nst[LAM0] = top_reverse(in_grid(whole(0)), nst[KAY0], nst[SLP0], nst[LAM1])
     reverse(1, T1, L2, L1)
-    total = surface(L3) + surface(L2)
     arrive(L2)
     reverse_faces(1, T1, L2, L1)
     add_delta(L1)
     send(L1)
-    total = total + surface(L1)
-    post(2, scatter(SOURCE * total, hot_e, e_high, 8))
     reverse(0, T0, L1, None)
+    flux_ref[...] = scatter(collect(2, 8), hot_p, p_high, 64)
     arrive(L1)
     reverse_faces(0, T0, L1, None)
     add_delta(None)
-    flux_ref[...] = scatter(collect(2), hot_p, p_high, 64)
+    overlay()
 
     for n in range(3):
         everything(n).wait_send()
     for f in range(7):
         sent(f)
+    for sends, _, c in tops:
+        when(sends, c.wait_send)
 
 
 def shards(state, diffusivity, patches, entries, table, sensitivity):
@@ -394,13 +580,18 @@
             pltpu.VMEM((2, CX, CZ), f32),
             pltpu.VMEM((3, NG * NB, 128), f32),
             pltpu.VMEM((3, NG * NB, 128), f32),
+            pltpu.VMEM((128, 8 * TL), bf16),
             pltpu.VMEM((128, 1024), bf16),
-            pltpu.VMEM((128, 1024), bf16),
+            pltpu.VMEM((4, 6, WY, 128), f32),
+            pltpu.VMEM((5, TR, 128), f32),
+            pltpu.VMEM((128, TL), f32),
             pltpu.SemaphoreType.DMA((3, 3)),
             pltpu.SemaphoreType.DMA((7, 4)),
             pltpu.SemaphoreType.DMA((7, 4)),
             pltpu.SemaphoreType.DMA((3,)),
             pltpu.SemaphoreType.DMA((3,)),
+            pltpu.SemaphoreType.DMA((9,)),
+            pltpu.SemaphoreType.DMA((9,)),
         ],
         compiler_params=pltpu.CompilerParams(
             collective_id=0, has_side_effects=True, vmem_limit_bytes=63 * 1024 * 1024),

time: 50.8 us -> 47.7 us (0.939)
  the two profiles are of different devices: /device:TPU:1 before, /device:TPU:0 now
where the time goes in v2:
time: 47.7 us; the launch traced here: 47.4 us
  Pallas kernels  43.1 us (90%)
  local copies, waits for them, and re-layouts  3.68 us (8%)
  between operations  0.64 us (1%)
    pallas_call x1, Pallas kernels, shards(): pl.pallas_call(kernel, out_shape=(jax.ShapeDtypeStruct((64, 128), f32), j...  43.1 us
    unnamed x2, local copies, waits for them, and re-layouts  3.68 us

profile of v2, /device:TPU:0, one launch (start us, length us, event | category | flops | bytes accessed | tf_op | source)
XLA Modules:
  0.0 47.4 jit_solution(2662452595547700486)
XLA Ops:
  0.6 43.1 %shard_map.77 = (f32[64,128]{1,0:T(8,128)}, f32[32,32,256]{2,1,0:T(8,128)}) custom-call(f32[32,32,256]{2,1,0:T(8,128)} %t0_hbm.1, f32[32,32,256]{2,1,0:T(8,128)} %d_hbm.1, f32[32,32,256]{2,1,0:T(8,128)} %l3_hbm.1, f32[64,128]{1,0:T(8,128)} %bitcast.5, s32[32,32]{1,0:T(8,128)} %entry_ref.1, s32[8,128]{1,0:T(8,128)} %bitcast.7), custom_call_target="tpu_custom_call" | custom-call | tf_op jit(solution)/shard_map/pallas_call | solution.py:563
  43.7 1.4 %copy.10 = f32[8192]{0:T(1024)} copy(f32[8192]{0:T(1024)} %bitcast.6) | data formatting | bytes 65536
  45.1 2.3 %copy.11 = f32[32,32,256]{2,1,0:T(8,128)} copy(f32[32,32,256]{2,1,0:T(8,128)} %get-tuple-element.9) | data formatting | bytes 2097152

commit v3 on v2

--- a/solution.py
+++ b/solution.py
@@ -37,8 +37,8 @@
 def kernel(
     t0_hbm, d_hbm, l3_hbm, patch_ref, entry_ref, table_ref,
     flux_ref, adj_ref,
-    fld, kay, slp, yrecv, ysend, kyh, kyf, syf, delta, outbox, inbox, hot_n, hot_p, top, nst, turn,
-    load_sem, xs_sem, xr_sem, a_send, a_recv, t_send, t_recv,
+    fld, kay, slp, yrecv, ysend, kyh, kyf, syf, delta, outbox, inbox, rows, gath, hot_n, hot_p, top, nst, turn,
+    load_sem, xs_sem, xr_sem, a_send, a_recv, g_send, g_recv, b_send, b_recv, t_send, t_recv,
 ):
     g = lax.axis_index("gx")
     b = lax.axis_index("bulk")
@@ -63,16 +63,69 @@
 
     def each_other(act):
         for j in range(1, NB):
-            act(g, lax.rem(b + j, NB))
+            act(g, ((b + j) & (NB - 1)))
 
         def body(i, _):
             for j in range(NB):
-                act(lax.rem(g + i, NG), lax.rem(b + j, NB))
+                act(((g + i) & (NG - 1)), ((b + j) & (NB - 1)))
             return 0
         lax.fori_loop(1, NG, body, 0)
 
-    each_other(lambda tg, tb: pl.semaphore_signal(
-        barrier, inc=1, device_id=(tg, tb), device_id_type=MESH))
+    for k in range(1, NG):
+        pl.semaphore_signal(barrier, inc=1, device_id=(((g + k) & (NG - 1)), b), device_id_type=MESH)
+    for k in range(1, NB):
+        pl.semaphore_signal(barrier, inc=1, device_id=(g, ((b + k) & (NB - 1))), device_id_type=MESH)
+    corners = [(i, j) for i in (1, NG - 1) for j in (1, NB - 1)]
+    for i, j in corners:
+        pl.semaphore_signal(
+            barrier, inc=1, device_id=(((g + i) & (NG - 1)), ((b + j) & (NB - 1))), device_id_type=MESH)
+
+    def swap(a):
+        lane, sub = iota((8, 128), 1), iota((8, 128), 0)
+        out = jnp.zeros((8, 128), jnp.float32)
+        for k in range(8):
+            turned = pltpu.roll(a, 16 * k, axis=1) if k else a
+            kept = jnp.where((lane >> 4) == sub, turned, 0.0)
+            out = out + (pltpu.roll(kept, 8 - k, axis=0) if k else kept)
+        return out
+
+    def stage_one(block):
+        rows[0] = block
+        rows[1, pl.ds(g, 1)] = rows[0, pl.ds(g, 1)]
+        copies = []
+        for k in range(1, NG):
+            o = ((g + k) & (NG - 1))
+            c = pltpu.make_async_remote_copy(
+                src_ref=rows.at[0, pl.ds(o, 1)], dst_ref=rows.at[1, pl.ds(g, 1)],
+                send_sem=g_send.at[k], recv_sem=g_recv.at[k],
+                device_id=(o, b), device_id_type=MESH)
+            c.start()
+            copies.append(c)
+        return copies
+
+    def stage_two(first):
+        for c in first:
+            c.wait_recv()
+        copies = []
+        for k in range(1, NB):
+            c = pltpu.make_async_remote_copy(
+                src_ref=rows.at[1], dst_ref=gath.at[b],
+                send_sem=b_send.at[k], recv_sem=b_recv.at[k],
+                device_id=(g, ((b + k) & (NB - 1))), device_id_type=MESH)
+            c.start()
+            copies.append(c)
+        gath[b] = rows[1]
+        return copies
+
+    def finish(second):
+        for c in second:
+            c.wait_recv()
+        lane = iota((8, 128), 1)
+        out = jnp.zeros((8, 128), jnp.float32)
+        for k in range(NB):
+            turned = pltpu.roll(gath[k], lax.rem(k - b + 128, 128), axis=1)
+            out = out + jnp.where((lane & 15) == k, turned, 0.0)
+        return swap(out)
 
     def post(n, block):
         pad = jnp.zeros((128 - block.shape[0], 128), jnp.float32)
@@ -467,27 +520,21 @@
             adj_ref[x, :, 0:128] = jnp.where(lane < 5, rows, adj_ref[x, :, 0:128])
 
     zero_edges()
-    table = table_ref[...].astype(jnp.float32)
-    pl.semaphore_wait(barrier, NG * NB - 1)
-    post(0, table)
+    table = swap(table_ref[...].astype(jnp.float32))
+    pl.semaphore_wait(barrier, NG - 1 + NB - 1 + len(corners))
+    first = stage_one(table)
     for i, f in ((0, T0), (1, DD), (2, L3)):
         for load in edge_loads[i]:
             load.wait()
         loads[i].wait()
-        send(f)
+        if f != L3:
+            send(f)
+    conduct(0, T0)
+    conduct_own(0, T0)
+    second = stage_two(first)
     top_pack()
     tops = top_copies()
-    for sends, _, c in tops:
-        when(sends, c.start)
-    conduct(0, T0)
-    conduct_own(0, T0)
-    patches = split3(patch_ref[...])
-
-    spot = collect(0, 8).astype(jnp.int32)
-    p_high = spot >> 7
-    make_hot(hot_p, spot & 127)
-    post(1, neighbours(lookup(patches, hot_p, p_high, 64)))
-
+    send(L3)
     forward(0, T0, T1)
     arrive(T0)
     arrive(DD)
@@ -495,9 +542,24 @@
     forward_faces(0, T0, T1)
     add_delta(T1)
     send(T1)
+    for sends, _, c in tops:
+        when(sends, c.start)
+    patches = split3(patch_ref[...])
+
+    spot = finish(second).astype(jnp.int32)
+    p_high = spot >> 7
+    make_hot(hot_p, spot & 127)
+    post(0, neighbours(lookup(patches, hot_p, p_high, 64)))
+
     conduct(1, T1)
     conduct_own(1, T1)
     forward(1, T1, T2)
+
+    arrive(T1)
+    conduct_halo(1, T1)
+    forward_faces(1, T1, T2)
+    add_delta(T2)
+    send(T2)
 
     for _, receives, c in tops:
         when(receives, c.wait_recv)
@@ -510,22 +572,6 @@
     nst[KAY0], nst[SLP0] = k0, s0
     nst[TEM1] = top_forward(t0, k0)
 
-    arrive(T1)
-    conduct_halo(1, T1)
-    forward_faces(1, T1, T2)
-    add_delta(T2)
-    send(T2)
-
-    heat = SOURCE * top_heat(collect(1, 72), entry)
-    t1 = in_grid(nst[TEM1] + heat)
-    k1, s1 = top_conduct(t1, d)
-    t2 = in_grid(top_forward(t1, k1) + heat)
-    k2, s2 = top_conduct(t2, d)
-    l2 = top_reverse(t2, k2, s2, l3)
-    l1 = top_reverse(t1, k1, s1, l2)
-    post(2, top_slots(SOURCE * (l3 + l2 + l1), entry))
-    nst[LAM1] = l1
-
     conduct(2, T2)
     conduct_own(2, T2)
     reverse(2, T2, L3, L2)
@@ -535,6 +581,16 @@
     reverse_faces(2, T2, L3, L2)
     add_delta(L2)
     send(L2)
+    heat = SOURCE * top_heat(collect(0, 72), entry)
+    t1 = in_grid(nst[TEM1] + heat)
+    k1, s1 = top_conduct(t1, d)
+    t2 = in_grid(top_forward(t1, k1) + heat)
+    k2, s2 = top_conduct(t2, d)
+    l2 = top_reverse(t2, k2, s2, l3)
+    l1 = top_reverse(t1, k1, s1, l2)
+    post(1, top_slots(SOURCE * (l3 + l2 + l1), entry))
+    nst[LAM1] = l1
+
     nst[LAM0] = top_reverse(in_grid(whole(0)), nst[KAY0], nst[SLP0], nst[LAM1])
     reverse(1, T1, L2, L1)
     arrive(L2)
@@ -542,14 +598,16 @@
     add_delta(L1)
     send(L1)
     reverse(0, T0, L1, None)
-    flux_ref[...] = scatter(collect(2, 8), hot_p, p_high, 64)
+    flux_ref[...] = scatter(collect(1, 8), hot_p, p_high, 64)
     arrive(L1)
     reverse_faces(0, T0, L1, None)
     add_delta(None)
     overlay()
 
-    for n in range(3):
+    for n in range(2):
         everything(n).wait_send()
+    for c in first + second:
+        c.wait_send()
     for f in range(7):
         sent(f)
     for sends, _, c in tops:
@@ -578,8 +636,10 @@
             pltpu.VMEM((3, 2, CX, CZ), f32),
             pltpu.VMEM((3, 2, CX, CZ), f32),
             pltpu.VMEM((2, CX, CZ), f32),
-            pltpu.VMEM((3, NG * NB, 128), f32),
-            pltpu.VMEM((3, NG * NB, 128), f32),
+            pltpu.VMEM((2, NG * NB, 128), f32),
+            pltpu.VMEM((2, NG * NB, 128), f32),
+            pltpu.VMEM((2, 8, 128), f32),
+            pltpu.VMEM((NB, 8, 128), f32),
             pltpu.VMEM((128, 8 * TL), bf16),
             pltpu.VMEM((128, 1024), bf16),
             pltpu.VMEM((4, 6, WY, 128), f32),
@@ -590,11 +650,15 @@
             pltpu.SemaphoreType.DMA((7, 4)),
             pltpu.SemaphoreType.DMA((3,)),
             pltpu.SemaphoreType.DMA((3,)),
+            pltpu.SemaphoreType.DMA((NG,)),
+            pltpu.SemaphoreType.DMA((NG,)),
+            pltpu.SemaphoreType.DMA((NB,)),
+            pltpu.SemaphoreType.DMA((NB,)),
             pltpu.SemaphoreType.DMA((9,)),
             pltpu.SemaphoreType.DMA((9,)),
         ],
         compiler_params=pltpu.CompilerParams(
-            collective_id=0, has_side_effects=True, vmem_limit_bytes=63 * 1024 * 1024),
+            collective_id=0, has_side_effects=True, vmem_limit_bytes=52 * 1024 * 1024),
     )(
         state, diffusivity, sensitivity, patches.reshape(64, 128),
         entries, jnp.swapaxes(table[0], 0, 1),

time: 47.7 us -> 44.1 us (0.925)
  the two profiles are of different devices: /device:TPU:0 before, /device:TPU:1 now
where the time goes in v3:
time: 44.1 us; the launch traced here: 43.6 us
  Pallas kernels  39.3 us (89%)
  local copies, waits for them, and re-layouts  3.74 us (8%)
  between operations  0.65 us (1%)
    pallas_call x1, Pallas kernels, shards(): pl.pallas_call(kernel, out_shape=(jax.ShapeDtypeStruct((64, 128), f32), j...  39.3 us
    unnamed x8, local copies, waits for them, and re-layouts  3.74 us

profile of v3, /device:TPU:1, one launch (start us, length us, event | category | flops | bytes accessed | tf_op | source)
XLA Modules:
  0.0 43.6 jit_solution(17491987218076494287)
XLA Ops:
  0.6 0.0 copy-start
  0.6 0.7 %copy-done = f32[8192]{0:T(1024)S(1)} copy-done((f32[8192]{0:T(1024)S(1)}, f32[8192]{0:T(1024)}, u32[]{:S(2)}) %copy-start) | copy-done | bytes 32792
  1.4 0.0 copy-start.1
  1.4 0.7 %copy-done.1 = s32[32,32]{1,0:T(8,128)S(1)} copy-done((s32[32,32]{1,0:T(8,128)S(1)}, s32[32,32]{1,0:T(8,128)}, u32[]{:S(2)}) %copy-start.1) | copy-done | bytes 4120
  2.1 0.0 copy-start.2
  2.1 0.7 %copy-done.2 = s32[1,128,8]{1,2,0:T(8,128)S(1)} copy-done((s32[1,128,8]{1,2,0:T(8,128)S(1)}, s32[1,128,8]{1,2,0:T(8,128)}, u32[]{:S(2)}) %copy-start.2) | copy-done | bytes 4120
  2.8 39.3 %shard_map.77 = (f32[64,128]{1,0:T(8,128)S(1)}, f32[32,32,256]{2,1,0:T(8,128)S(1)}) custom-call(f32[32,32,256]{2,1,0:T(8,128)} %t0_hbm.1, f32[32,32,256]{2,1,0:T(8,128)} %d_hbm.1, f32[32,32,256]{2,1,0:T(8,128)} %l3_hbm.1, f32[64,128]{1,0:T(8,128)S(1)} %bitcast.5, s32[32,32]{1,0:T(8,128)S(1)} %copy-done.1, s32[8,128]{1,0:T(8,128)S(1)} %bitcast.7), custom_call_target="tpu_custom_call" | custom-call | tf_op jit(solution)/shard_map/pallas_call | solution.py:621
  42.1 0.6 %copy.10 = f32[8192]{0:T(1024)} copy(f32[8192]{0:T(1024)S(1)} %bitcast.6) | data formatting | bytes 65536
  42.7 1.0 %copy.11 = f32[32,32,256]{2,1,0:T(8,128)} copy(f32[32,32,256]{2,1,0:T(8,128)S(1)} %get-tuple-element.9) | data formatting | bytes 2097152
Async XLA Ops:
  0.6 0.8 %copy-start = (f32[8192]{0:T(1024)S(1)}, f32[8192]{0:T(1024)}, u32[]{:S(2)}) copy-start(f32[8192]{0:T(1024)} %param.8) | copy-start | bytes 98308
  1.4 0.7 %copy-start.1 = (s32[32,32]{1,0:T(8,128)S(1)}, s32[32,32]{1,0:T(8,128)}, u32[]{:S(2)}) copy-start(s32[32,32]{1,0:T(8,128)} %entry_ref.1) | copy-start | bytes 12292
  2.1 0.7 %copy-start.2 = (s32[1,128,8]{1,2,0:T(8,128)S(1)}, s32[1,128,8]{1,2,0:T(8,128)}, u32[]{:S(2)}) copy-start(s32[1,128,8]{1,2,0:T(8,128)} %param.10) | copy-start | bytes 12292

commit v4 on v3

--- a/solution.py
+++ b/solution.py
@@ -531,11 +531,11 @@
             send(f)
     conduct(0, T0)
     conduct_own(0, T0)
-    second = stage_two(first)
     top_pack()
     tops = top_copies()
     send(L3)
     forward(0, T0, T1)
+    second = stage_two(first)
     arrive(T0)
     arrive(DD)
     conduct_halo(0, T0)
@@ -591,12 +591,12 @@
     post(1, top_slots(SOURCE * (l3 + l2 + l1), entry))
     nst[LAM1] = l1
 
-    nst[LAM0] = top_reverse(in_grid(whole(0)), nst[KAY0], nst[SLP0], nst[LAM1])
     reverse(1, T1, L2, L1)
     arrive(L2)
     reverse_faces(1, T1, L2, L1)
     add_delta(L1)
     send(L1)
+    nst[LAM0] = top_reverse(in_grid(whole(0)), nst[KAY0], nst[SLP0], nst[LAM1])
     reverse(0, T0, L1, None)
     flux_ref[...] = scatter(collect(1, 8), hot_p, p_high, 64)
     arrive(L1)

time: 44.1 us -> 43.3 us (0.982)
  Pallas kernels: 39.3 us -> 38.6 us
    pallas_call x1, Pallas kernels: 39.3 us -> 38.6 us  [shards(): pl.pallas_call(kernel, out_shape=(jax.ShapeDtypeStruct((64, 128), f32), j...]
where the time goes in v4:
time: 43.3 us; the launch traced here: 43 us
  Pallas kernels  38.6 us (89%)
  local copies, waits for them, and re-layouts  3.74 us (9%)
  between operations  0.65 us (2%)
    pallas_call x1, Pallas kernels, shards(): pl.pallas_call(kernel, out_shape=(jax.ShapeDtypeStruct((64, 128), f32), j...  38.6 us
    unnamed x8, local copies, waits for them, and re-layouts  3.74 us

profile of v4, /device:TPU:1, one launch (start us, length us, event | category | flops | bytes accessed | tf_op | source)
XLA Modules:
  0.0 43.0 jit_solution(14571345434685103600)
XLA Ops:
  0.6 0.0 copy-start
  0.6 0.7 %copy-done = f32[8192]{0:T(1024)S(1)} copy-done((f32[8192]{0:T(1024)S(1)}, f32[8192]{0:T(1024)}, u32[]{:S(2)}) %copy-start) | copy-done | bytes 32792
  1.4 0.0 copy-start.1
  1.4 0.7 %copy-done.1 = s32[32,32]{1,0:T(8,128)S(1)} copy-done((s32[32,32]{1,0:T(8,128)S(1)}, s32[32,32]{1,0:T(8,128)}, u32[]{:S(2)}) %copy-start.1) | copy-done | bytes 4120
  2.1 0.0 copy-start.2
  2.1 0.7 %copy-done.2 = s32[1,128,8]{1,2,0:T(8,128)S(1)} copy-done((s32[1,128,8]{1,2,0:T(8,128)S(1)}, s32[1,128,8]{1,2,0:T(8,128)}, u32[]{:S(2)}) %copy-start.2) | copy-done | bytes 4120
  2.8 38.6 %shard_map.77 = (f32[64,128]{1,0:T(8,128)S(1)}, f32[32,32,256]{2,1,0:T(8,128)S(1)}) custom-call(f32[32,32,256]{2,1,0:T(8,128)} %t0_hbm.1, f32[32,32,256]{2,1,0:T(8,128)} %d_hbm.1, f32[32,32,256]{2,1,0:T(8,128)} %l3_hbm.1, f32[64,128]{1,0:T(8,128)S(1)} %bitcast.5, s32[32,32]{1,0:T(8,128)S(1)} %copy-done.1, s32[8,128]{1,0:T(8,128)S(1)} %bitcast.7), custom_call_target="tpu_custom_call" | custom-call | tf_op jit(solution)/shard_map/pallas_call | solution.py:621
  41.4 0.6 %copy.10 = f32[8192]{0:T(1024)} copy(f32[8192]{0:T(1024)S(1)} %bitcast.6) | data formatting | bytes 65536
  42.1 1.0 %copy.11 = f32[32,32,256]{2,1,0:T(8,128)} copy(f32[32,32,256]{2,1,0:T(8,128)S(1)} %get-tuple-element.9) | data formatting | bytes 2097152
Async XLA Ops:
  0.6 0.8 %copy-start = (f32[8192]{0:T(1024)S(1)}, f32[8192]{0:T(1024)}, u32[]{:S(2)}) copy-start(f32[8192]{0:T(1024)} %param.8) | copy-start | bytes 98308
  1.4 0.7 %copy-start.1 = (s32[32,32]{1,0:T(8,128)S(1)}, s32[32,32]{1,0:T(8,128)}, u32[]{:S(2)}) copy-start(s32[32,32]{1,0:T(8,128)} %entry_ref.1) | copy-start | bytes 12292
  2.1 0.7 %copy-start.2 = (s32[1,128,8]{1,2,0:T(8,128)S(1)}, s32[1,128,8]{1,2,0:T(8,128)}, u32[]{:S(2)}) copy-start(s32[1,128,8]{1,2,0:T(8,128)} %param.10) | copy-start | bytes 12292

commit v5 on v4

--- a/solution.py
+++ b/solution.py
@@ -54,11 +54,6 @@
         pltpu.make_async_copy(src, fld.at[f, pl.ds(1, CX)], load_sem.at[f, 2])
         for f, src in inputs
     ]
-    for pair in edge_loads:
-        for load in pair:
-            load.start()
-    for load in loads:
-        load.start()
     barrier = pltpu.get_barrier_semaphore()
 
     def each_other(act):
@@ -79,6 +74,12 @@
     for i, j in corners:
         pl.semaphore_signal(
             barrier, inc=1, device_id=(((g + i) & (NG - 1)), ((b + j) & (NB - 1))), device_id_type=MESH)
+
+    for pair in edge_loads:
+        for load in pair:
+            load.start()
+    for load in loads:
+        load.start()
 
     def swap(a):
         lane, sub = iota((8, 128), 1), iota((8, 128), 0)

time: 43.3 us -> 43 us (level)
  no operation moved by 1% of the time
where the time goes in v5:
time: 43 us; the launch traced here: 42.7 us
  Pallas kernels  38.3 us (89%)
  local copies, waits for them, and re-layouts  3.74 us (9%)
  between operations  0.65 us (2%)
    pallas_call x1, Pallas kernels, shards(): pl.pallas_call(kernel, out_shape=(jax.ShapeDtypeStruct((64, 128), f32), j...  38.3 us
    unnamed x8, local copies, waits for them, and re-layouts  3.74 us

profile of v5, /device:TPU:1, one launch (start us, length us, event | category | flops | bytes accessed | tf_op | source)
XLA Modules:
  0.0 42.7 jit_solution(13681389632366378313)
XLA Ops:
  0.6 0.0 copy-start
  0.6 0.7 %copy-done = f32[8192]{0:T(1024)S(1)} copy-done((f32[8192]{0:T(1024)S(1)}, f32[8192]{0:T(1024)}, u32[]{:S(2)}) %copy-start) | copy-done | bytes 32792
  1.4 0.0 copy-start.1
  1.4 0.7 %copy-done.1 = s32[32,32]{1,0:T(8,128)S(1)} copy-done((s32[32,32]{1,0:T(8,128)S(1)}, s32[32,32]{1,0:T(8,128)}, u32[]{:S(2)}) %copy-start.1) | copy-done | bytes 4120
  2.1 0.0 copy-start.2
  2.1 0.7 %copy-done.2 = s32[1,128,8]{1,2,0:T(8,128)S(1)} copy-done((s32[1,128,8]{1,2,0:T(8,128)S(1)}, s32[1,128,8]{1,2,0:T(8,128)}, u32[]{:S(2)}) %copy-start.2) | copy-done | bytes 4120
  2.8 38.3 %shard_map.77 = (f32[64,128]{1,0:T(8,128)S(1)}, f32[32,32,256]{2,1,0:T(8,128)S(1)}) custom-call(f32[32,32,256]{2,1,0:T(8,128)} %t0_hbm.1, f32[32,32,256]{2,1,0:T(8,128)} %d_hbm.1, f32[32,32,256]{2,1,0:T(8,128)} %l3_hbm.1, f32[64,128]{1,0:T(8,128)S(1)} %bitcast.5, s32[32,32]{1,0:T(8,128)S(1)} %copy-done.1, s32[8,128]{1,0:T(8,128)S(1)} %bitcast.7), custom_call_target="tpu_custom_call" | custom-call | tf_op jit(solution)/shard_map/pallas_call | solution.py:622
  41.1 0.6 %copy.10 = f32[8192]{0:T(1024)} copy(f32[8192]{0:T(1024)S(1)} %bitcast.6) | data formatting | bytes 65536
  41.8 1.0 %copy.11 = f32[32,32,256]{2,1,0:T(8,128)} copy(f32[32,32,256]{2,1,0:T(8,128)S(1)} %get-tuple-element.9) | data formatting | bytes 2097152
Async XLA Ops:
  0.6 0.8 %copy-start = (f32[8192]{0:T(1024)S(1)}, f32[8192]{0:T(1024)}, u32[]{:S(2)}) copy-start(f32[8192]{0:T(1024)} %param.8) | copy-start | bytes 98308
  1.4 0.7 %copy-start.1 = (s32[32,32]{1,0:T(8,128)S(1)}, s32[32,32]{1,0:T(8,128)}, u32[]{:S(2)}) copy-start(s32[32,32]{1,0:T(8,128)} %entry_ref.1) | copy-start | bytes 12292
  2.1 0.7 %copy-start.2 = (s32[1,128,8]{1,2,0:T(8,128)S(1)}, s32[1,128,8]{1,2,0:T(8,128)}, u32[]{:S(2)}) copy-start(s32[1,128,8]{1,2,0:T(8,128)} %param.10) | copy-start | bytes 12292
